TPU v7x, 32 devices: a whole 2x2x4 slice. The times are simulated.
32 devices in a mesh: blk: 8 (over z, x), blade: 4 (over y, core).
Axes of the slice: x: 2, y: 2, z: 4, core: 2. Of those that a mesh axis runs over, the one named last changes fastest.
Arguments:
- bnd_pos: float32 [3, 2048], P(None, 'blk'), may hold values from -1 to 1
- bnd_owner: int32 [2048, 1], P('blk'), may hold values from 0 to 7; in each aligned block of 256 rows (0 to 255, 256 to 511, ...) at most 64 rows name the same one
- bnd_slot: int32 [2048], P('blk'), may hold values from 0 to 16383
- seg_start: float32 [3, 4, 1024], P(None, 'blade', 'blk'), may hold values from -1 to 1
- seg_step: float32 [3, 4, 1024], P(None, 'blade', 'blk'), may hold values from -0.15 to 0.15
- seg_gamma: float32 [4, 1024], P('blade', 'blk'), may hold values from -6 to 6
- seg_sec: int32 [4, 1024], P('blade', 'blk'), may hold values from 0 to 63
- flow: float32 [3, 64, 64, 256], P(None, 'blk', 'blade'), may hold values from -6 to 6
- source: float32 [3, 64, 64, 256], P(None, 'blk', 'blade'), may hold values from -6 to 6
- extra_diag: float32 [64, 64, 256], P('blk', 'blade'), may hold values from 0.25 to 2
- circ_weight: float32 [64, 64, 256], P('blk', 'blade'), may hold values from -0.125 to 0.125
- sec_block: int32 [4, 64], replicated, may hold values from 0 to 7
- sec_row: int32 [4, 64], replicated, may hold values from 0 to 15
Outputs:
- new_flow: float32 [3, 64, 64, 256], P(None, 'blk', 'blade')
- new_gamma: float32 [4, 1024], P('blade', 'blk')
Inputs may be any that keep to these rules, and one draw needn't show every extreme that they name: `bnd_owner`: among the 256 boundary cells of each aligned block (one index of blk), at most 64 have the same owner, and some owner has exactly 64.
All inputs are finite; a program needn't handle non-finite values.
Results may differ from a plain program's by a relative error of at most 0.0001.
Values sent between devices are 32-bit elements; how exact they have to be, the bound alone decides.
A program may use at most 64 MiB of HBM per device.

v0:
```python
import math
import jax
import jax.numpy as jnp
from jax import lax
from jax.sharding import PartitionSpec as P

PASSES = 2
CORE = 0.01
FOUR_PI = 4.0 * math.pi
OMEGA = 0.8
RELAX = 0.5


def with_halo(array, sides, width):
    for axis, dim in sides:
        size, length = (lax.axis_size(axis), array.shape[dim])
        up = [(i, (i + 1) % size) for i in range(size - 1)]
        down = [(j, i) for i, j in up]
        last = lax.slice_in_dim(array, length - width, length, axis=dim)
        leading = lax.slice_in_dim(array, 0, width, axis=dim)
        before = lax.ppermute(last, axis, up)
        after = lax.ppermute(leading, axis, down)
        array = jnp.concatenate([before, array, after], axis=dim)
    return array


def pair_velocity(points, segs):
    p = points[:, :, None]
    start = segs[0:3, None, :]
    step = segs[3:6, None, :]
    gamma = segs[6][None, :]
    r1 = p - start
    r2 = r1 - step
    cross_x = r1[1] * r2[2] - r1[2] * r2[1]
    cross_y = r1[2] * r2[0] - r1[0] * r2[2]
    cross_z = r1[0] * r2[1] - r1[1] * r2[0]
    cross_sq = cross_x * cross_x + cross_y * cross_y + cross_z * cross_z
    norm_one = jnp.sqrt(jnp.sum(r1 * r1, 0) + CORE)
    norm_two = jnp.sqrt(jnp.sum(r2 * r2, 0) + CORE)
    step_sq = jnp.sum(step * step, 0)
    along = jnp.sum(step * (r1 / norm_one - r2 / norm_two), 0)
    weight = gamma * along / (FOUR_PI * (cross_sq + CORE * step_sq + CORE * CORE))
    return jnp.stack(
        [jnp.sum(weight * cross_x, 1), jnp.sum(weight * cross_y, 1), jnp.sum(weight * cross_z, 1)]
    )


def spanned(points, segs, width):
    count = segs.shape[1]
    if count > width and count % width == 0:

        def add_part(index, total):
            part = lax.dynamic_slice_in_dim(segs, index * width, width, 1)
            return total + pair_velocity(points, part)

        return lax.fori_loop(
            0, count // width, add_part, jnp.zeros((3, points.shape[1]), jnp.float32)
        )
    return pair_velocity(points, segs)


def sweep(padded, rhs, dgl):
    zpad = jnp.pad(padded, ((0, 0), (0, 0), (0, 0), (1, 1)))
    center = padded[:, 1:-1, 1:-1, :]
    beside = zpad[:, 2:, 1:-1, 1:-1] + zpad[:, :-2, 1:-1, 1:-1]
    beside = beside + zpad[:, 1:-1, 2:, 1:-1] + zpad[:, 1:-1, :-2, 1:-1]
    beside = beside + zpad[:, 1:-1, 1:-1, 2:] + zpad[:, 1:-1, 1:-1, :-2]
    resid = rhs - (dgl * center - beside)
    return center + OMEGA * resid / dgl


def per_device(
    bnd_pos,
    bnd_owner,
    bnd_slot,
    seg_start,
    seg_step,
    seg_gamma,
    seg_sec,
    flow,
    source,
    extra_diag,
    circ_weight,
    sec_block,
    sec_row,
):
    n_blk = lax.axis_size("blk")
    cells = bnd_pos.shape[1]
    cap = max(2, 2 * cells // n_blk)
    depth_y = flow.shape[2]
    depth_z = flow.shape[3]
    own_wake = jnp.concatenate([seg_start[:, 0], seg_step[:, 0], seg_gamma], 0)
    partial_value = spanned(bnd_pos, lax.all_gather(own_wake, "blk", axis=1, tiled=True), 2048)
    velocity = lax.psum(partial_value, "blade")
    owner = bnd_owner[:, 0]
    onehot = (owner[:, None] == jnp.arange(n_blk, dtype=jnp.int32)[None, :]).astype(jnp.int32)
    rank = jnp.sum(jnp.cumsum(onehot, 0) * onehot, 1) - 1
    where_to = owner * cap + rank
    payload = jnp.concatenate([velocity, bnd_slot.astype(jnp.float32)[None]], 0)
    outgoing = (
        jnp.zeros((4, n_blk * cap), jnp.float32).at[:, where_to].set(payload).reshape(4, n_blk, cap)
    )
    incoming = lax.all_to_all(outgoing, "blk", split_axis=1, concat_axis=1, tiled=True).reshape(
        4, n_blk * cap
    )
    slot = incoming[3].astype(jnp.int32)
    blade_index = lax.axis_index("blade")
    local_y = slot // depth_z - blade_index * depth_y
    local_z = slot % depth_z
    keep = (local_y >= 0) & (local_y < depth_y)
    values = jnp.where(keep[None, :], incoming[:3], 0.0)
    face = (
        jnp.zeros((3, depth_y, depth_z), jnp.float32)
        .at[:, jnp.clip(local_y, 0, depth_y - 1), local_z]
        .add(values)
    )
    rhs = source.at[:, 0].add(face)
    dgl = 6.0 + extra_diag
    state = flow
    for step in range(PASSES):
        padded = with_halo(state, (("blk", 1), ("blade", 2)), 1)
        state = sweep(padded, rhs, dgl)
    profile = jnp.sum(circ_weight * state[1], axis=(0, 2))
    profiles = lax.all_gather(profile[None], "blk", axis=0, tiled=True)
    block_row = lax.dynamic_index_in_dim(sec_block, blade_index, 0, keepdims=False)
    row_here = lax.dynamic_index_in_dim(sec_row, blade_index, 0, keepdims=False)
    section = profiles[block_row, row_here]
    nsec = section.shape[0]
    match = seg_sec[0][:, None] == jnp.arange(nsec, dtype=jnp.int32)[None, :]
    looked = jnp.sum(jnp.where(match, section[None, :], 0.0), 1)
    new_gamma = ((1.0 - RELAX) * seg_gamma[0] + RELAX * looked)[None]
    return (state, new_gamma)


def solution(mesh):
    return jax.shard_map(
        per_device,
        mesh=mesh,
        in_specs=(
            P(None, "blk"),
            P("blk", None),
            P("blk"),
            P(None, "blade", "blk"),
            P(None, "blade", "blk"),
            P("blade", "blk"),
            P("blade", "blk"),
            P(None, "blk", "blade", None),
            P(None, "blk", "blade", None),
            P("blk", "blade", None),
            P("blk", "blade", None),
            P(),
            P(),
        ),
        out_specs=(P(None, "blk", "blade", None), P("blade", "blk")),
        check_vma=False,
    )
```

profile of v0, /device:TPU:4, one launch (start us, length us, event | category | flops | bytes accessed | tf_op | source)
XLA Modules:
  0.0 136.4 jit_solution(2110822875356458950)
XLA Ops:
  0.6 0.7 copy_bitcast_fusion
  2.0 30.7 %all_gather.6 = f32[7,1024]{1,0:T(8,128)S(1)} all-gather(f32[7,128]{1,0:T(8,128)S(1)} %pad_maximum_fusion.15), channel_id=1, replica_groups=mesh['blk'=8,'blade'=4] {'blk'}, dimensions={1}, use_global_device_ids=true | all-gather | bytes 32256 | tf_op jit(solution)/shard_map/all_gather | solution.py:93
  32.8 1.7 %fusion.2 = (f32[256,1024]{1,0:T(8,128)S(1)}, f32[256,1024]{1,0:T(8,128)S(1)}, f32[3,256,1024]{2,1,0:T(8,128)S(1)}) fusion(f32[3,1024]{1,0:T(4,128)S(1)} %get-tuple-element.34, f32[3,256]{1,0:T(4,128)} %param.15, f32[3,1024]{1,0:T(4,128)S(1)} %get-tuple-element.35), kind=kLoop, calls=%fused_computation.8 | loop fusion | flops 4194304 | bytes 5270528 | tf_op jit(solution)/shard_map/reduce_sum | solution.py:38
  35.4 0.9 subtract_subtract_fusion
  36.3 1.4 fusion.9
  38.1 5.9 %psum.7 = f32[3,256]{1,0:T(4,128)S(1)} all-reduce(f32[3,256]{1,0:T(4,128)S(1)} %pad_maximum_fusion.16), channel_id=1, replica_groups=mesh['blk'=8,'blade'=4] {'blade'}, use_global_device_ids=true, to_apply=%region_10.11 | all-reduce | flops 768 | bytes 6144 | tf_op jit(solution)/shard_map/psum | solution.py:94
  45.1 1.2 scatter_custom_fusion
  47.2 5.5 %all-to-all-start = ((f32[8,1,256]{2,1,0:T(1,128)}), f32[8,1,256]{2,1,0:T(1,128)S(1)}, u32[]{:S(2)}, u32[]{:S(2)}) async-start(f32[8,1,256]{2,1,0:T(1,128)} %reshape.330), calls=%async_computation | async-start | bytes 16384 | tf_op jit(solution)/shard_map/all_to_all | solution.py:103
  52.6 3.9 %collective-permute-start.1 = (f32[3,1,16,256]{3,2,1,0:T(8,128)S(1)}, f32[3,1,16,256]{3,2,1,0:T(8,128)S(1)}, u32[]{:S(2)}, u32[]{:S(2)}) collective-permute-start(f32[3,1,16,256]{3,2,1,0:T(8,128)S(1)} %get-tuple-element.30), channel_id=1, source_target_pairs={{0,4},{4,8},{8,12},{12,16},{16,20},{20,24},{24,28},{1,5},{5,9},{9,... | collective-permute-start | bytes 147464 | tf_op jit(solution)/shard_map/ppermute | solution.py:21
  56.6 1.3 collective-permute-start
  57.9 1.2 all-to-all-done
  61.1 25.4 %scatter_fusion = f32[3,16,256]{0,2,1:T(8,128)S(1)} fusion(f32[3,16,256]{0,2,1:T(8,128)S(1)} %broadcast_in_dim.28, s32[512]{0:T(512)S(1)} %bitcast.90, f32[512,3]{1,0:T(8,128)S(1)} %copy.41), kind=kCustom, calls=%fused_computation.2 | custom fusion | flops 1536 | bytes 22528 | tf_op jit(solution)/shard_map/scatter-add | solution.py:115
  87.3 1.9 %collective-permute-start.2 = (f32[3,10,1,256]{3,2,1,0:T(1,128)S(1)}, f32[3,10,1,256]{3,2,1,0:T(1,128)S(1)}, u32[]{:S(2)}, u32[]{:S(2)}) collective-permute-start(f32[3,10,1,256]{3,2,1,0:T(1,128)S(1)} %get-tuple-element.26), channel_id=1, source_target_pairs={{1,0},{2,1},{3,2},{5,4},{6,5},{7,6},{9,8},{10,9},{11,10},{13,12},{... | collective-permute-start | bytes 92168 | tf_op jit(solution)/shard_map/ppermute | solution.py:22
  89.2 2.4 %collective-permute-start.3 = (f32[3,10,1,256]{3,2,1,0:T(1,128)S(1)}, f32[3,10,1,256]{3,2,1,0:T(1,128)S(1)}, u32[]{:S(2)}, u32[]{:S(2)}) collective-permute-start(f32[3,10,1,256]{3,2,1,0:T(1,128)S(1)} %get-tuple-element.25), channel_id=1, source_target_pairs={{0,1},{1,2},{2,3},{4,5},{5,6},{6,7},{8,9},{9,10},{10,11},{12,13},{... | collective-permute-start | bytes 92168 | tf_op jit(solution)/shard_map/ppermute | solution.py:21
  91.7 2.8 %collective-permute-done.3 = f32[3,10,1,256]{3,2,1,0:T(1,128)S(1)} collective-permute-done((f32[3,10,1,256]{3,2,1,0:T(1,128)S(1)}, f32[3,10,1,256]{3,2,1,0:T(1,128)S(1)}, u32[]{:S(2)}, u32[]{:S(2)}) %collective-permute-start.3) | collective-permute-done | bytes 30752 | tf_op jit(solution)/shard_map/ppermute | solution.py:21
  95.4 1.3 collective-permute-start.4
  96.7 4.5 %collective-permute-start.5 = (f32[3,1,16,256]{3,2,1,0:T(8,128)S(1)}, f32[3,1,16,256]{3,2,1,0:T(8,128)S(1)}, u32[]{:S(2)}, u32[]{:S(2)}) collective-permute-start(f32[3,1,16,256]{3,2,1,0:T(8,128)S(1)} %get-tuple-element.27), channel_id=1, source_target_pairs={{0,4},{4,8},{8,12},{12,16},{16,20},{20,24},{24,28},{1,5},{5,9},{9,... | collective-permute-start | bytes 147464 | tf_op jit(solution)/shard_map/ppermute | solution.py:21
  101.4 1.6 %collective-permute-done.5 = f32[3,1,16,256]{3,2,1,0:T(8,128)S(1)} collective-permute-done((f32[3,1,16,256]{3,2,1,0:T(8,128)S(1)}, f32[3,1,16,256]{3,2,1,0:T(8,128)S(1)}, u32[]{:S(2)}, u32[]{:S(2)}) %collective-permute-start.5) | collective-permute-done | bytes 49184 | tf_op jit(solution)/shard_map/ppermute | solution.py:21
  103.1 1.9 %collective-permute-start.6 = (f32[3,10,1,256]{3,2,1,0:T(1,128)S(1)}, f32[3,10,1,256]{3,2,1,0:T(1,128)S(1)}, u32[]{:S(2)}, u32[]{:S(2)}) collective-permute-start(f32[3,10,1,256]{3,2,1,0:T(1,128)S(1)} %get-tuple-element.24), channel_id=1, source_target_pairs={{1,0},{2,1},{3,2},{5,4},{6,5},{7,6},{9,8},{10,9},{11,10},{13,12},{... | collective-permute-start | bytes 92168 | tf_op jit(solution)/shard_map/ppermute | solution.py:22
  105.0 2.4 %collective-permute-start.7 = (f32[3,10,1,256]{3,2,1,0:T(1,128)S(1)}, f32[3,10,1,256]{3,2,1,0:T(1,128)S(1)}, u32[]{:S(2)}, u32[]{:S(2)}) collective-permute-start(f32[3,10,1,256]{3,2,1,0:T(1,128)S(1)} %get-tuple-element.23), channel_id=1, source_target_pairs={{0,1},{1,2},{2,3},{4,5},{5,6},{6,7},{8,9},{9,10},{10,11},{12,13},{... | collective-permute-start | bytes 92168 | tf_op jit(solution)/shard_map/ppermute | solution.py:21
  107.4 0.7 or_bitcast_fusion
  109.4 0.8 collective-permute-done.7
  112.1 22.8 %all-reduce.2 = f32[128]{0:T(128)S(1)} all-reduce(f32[128]{0:T(128)S(1)} %dynamic-update-slice.3), channel_id=2, replica_groups=mesh['blk'=8,'blade'=4] {'blk'}, use_global_device_ids=true, to_apply=%add.2 | all-reduce | flops 128 | bytes 1024
  135.0 0.7 gather_fusion
  (83 shorter events, 10.9 us)
Async XLA Ops:
  34.7 0.7 copy-start.5
  37.7 6.3 %copy-start.7 = (s32[256]{0:T(256)S(1)}, s32[256]{0:T(256)}, u32[]{:S(2)}) copy-start(s32[256]{0:T(256)} %param.17) | copy-start | bytes 3076
  37.7 6.5 %copy-start.6 = (s32[256,1]{0,1:T(1,128)S(1)}, s32[256,1]{0,1:T(1,128)}, u32[]{:S(2)}) copy-start(s32[256,1]{0,1:T(1,128)} %param.16) | copy-start | bytes 3076
  37.7 14.9 %copy-start.1 = (f32[3,8,16,256]{3,2,1,0:T(8,128)S(1)}, f32[3,8,16,256]{3,2,1,0:T(8,128)}, u32[]{:S(2)}) copy-start(f32[3,8,16,256]{3,2,1,0:T(8,128)} %param.22) | copy-start | bytes 1179652
  38.1 19.8 %copy-start.3 = (f32[8,16,256]{2,1,0:T(8,128)S(1)}, f32[8,16,256]{2,1,0:T(8,128)}, u32[]{:S(2)}) copy-start(f32[8,16,256]{2,1,0:T(8,128)} %param.24) | copy-start | bytes 393220
  47.2 12.0 %all-to-all-start = ((f32[8,1,256]{2,1,0:T(1,128)}), f32[8,1,256]{2,1,0:T(1,128)S(1)}, u32[]{:S(2)}, u32[]{:S(2)}) async-start(f32[8,1,256]{2,1,0:T(1,128)} %reshape.330), calls=%async_computation | async-start | bytes 16384 | tf_op jit(solution)/shard_map/all_to_all | solution.py:103
  52.6 34.5 %collective-permute-start.1 = (f32[3,1,16,256]{3,2,1,0:T(8,128)S(1)}, f32[3,1,16,256]{3,2,1,0:T(8,128)S(1)}, u32[]{:S(2)}, u32[]{:S(2)}) collective-permute-start(f32[3,1,16,256]{3,2,1,0:T(8,128)S(1)} %get-tuple-element.30), channel_id=1, source_target_pairs={{0,4},{4,8},{8,12},{12,16},{16,20},{20,24},{24,28},{1,5},{5,9},{9,... | collective-permute-start | bytes 147464 | tf_op jit(solution)/shard_map/ppermute | solution.py:21
  56.6 30.6 %collective-permute-start = (f32[3,1,16,256]{3,2,1,0:T(8,128)S(1)}, f32[3,1,16,256]{3,2,1,0:T(8,128)S(1)}, u32[]{:S(2)}, u32[]{:S(2)}) collective-permute-start(f32[3,1,16,256]{3,2,1,0:T(8,128)S(1)} %get-tuple-element.29), channel_id=1, source_target_pairs={{4,0},{8,4},{12,8},{16,12},{20,16},{24,20},{28,24},{5,1},{9,5},{13... | collective-permute-start | bytes 147464 | tf_op jit(solution)/shard_map/ppermute | solution.py:22
  86.5 5.1 %copy-start = (f32[3,8,16,256]{3,2,1,0:T(8,128)S(1)}, f32[3,8,16,256]{3,2,1,0:T(8,128)}, u32[]{:S(2)}) copy-start(f32[3,8,16,256]{3,2,1,0:T(8,128)} %param.23) | copy-start | bytes 1179652
  87.3 4.4 %collective-permute-start.2 = (f32[3,10,1,256]{3,2,1,0:T(1,128)S(1)}, f32[3,10,1,256]{3,2,1,0:T(1,128)S(1)}, u32[]{:S(2)}, u32[]{:S(2)}) collective-permute-start(f32[3,10,1,256]{3,2,1,0:T(1,128)S(1)} %get-tuple-element.26), channel_id=1, source_target_pairs={{1,0},{2,1},{3,2},{5,4},{6,5},{7,6},{9,8},{10,9},{11,10},{13,12},{... | collective-permute-start | bytes 92168 | tf_op jit(solution)/shard_map/ppermute | solution.py:22
  89.2 5.2 %collective-permute-start.3 = (f32[3,10,1,256]{3,2,1,0:T(1,128)S(1)}, f32[3,10,1,256]{3,2,1,0:T(1,128)S(1)}, u32[]{:S(2)}, u32[]{:S(2)}) collective-permute-start(f32[3,10,1,256]{3,2,1,0:T(1,128)S(1)} %get-tuple-element.25), channel_id=1, source_target_pairs={{0,1},{1,2},{2,3},{4,5},{5,6},{6,7},{8,9},{9,10},{10,11},{12,13},{... | collective-permute-start | bytes 92168 | tf_op jit(solution)/shard_map/ppermute | solution.py:21
  95.0 13.1 %copy-start.10 = (u32[32]{0:T(128)S(1)}, u32[32]{0:T(128)}, u32[]{:S(2)}) copy-start(u32[32]{0:T(128)} %constant.144) | copy-start | bytes 388
  95.4 6.0 %collective-permute-start.4 = (f32[3,1,16,256]{3,2,1,0:T(8,128)S(1)}, f32[3,1,16,256]{3,2,1,0:T(8,128)S(1)}, u32[]{:S(2)}, u32[]{:S(2)}) collective-permute-start(f32[3,1,16,256]{3,2,1,0:T(8,128)S(1)} %get-tuple-element.28), channel_id=1, source_target_pairs={{4,0},{8,4},{12,8},{16,12},{20,16},{24,20},{28,24},{5,1},{9,5},{13... | collective-permute-start | bytes 147464 | tf_op jit(solution)/shard_map/ppermute | solution.py:22
  96.7 6.3 %collective-permute-start.5 = (f32[3,1,16,256]{3,2,1,0:T(8,128)S(1)}, f32[3,1,16,256]{3,2,1,0:T(8,128)S(1)}, u32[]{:S(2)}, u32[]{:S(2)}) collective-permute-start(f32[3,1,16,256]{3,2,1,0:T(8,128)S(1)} %get-tuple-element.27), channel_id=1, source_target_pairs={{0,4},{4,8},{8,12},{12,16},{16,20},{20,24},{24,28},{1,5},{5,9},{9,... | collective-permute-start | bytes 147464 | tf_op jit(solution)/shard_map/ppermute | solution.py:21
  103.1 6.3 %collective-permute-start.6 = (f32[3,10,1,256]{3,2,1,0:T(1,128)S(1)}, f32[3,10,1,256]{3,2,1,0:T(1,128)S(1)}, u32[]{:S(2)}, u32[]{:S(2)}) collective-permute-start(f32[3,10,1,256]{3,2,1,0:T(1,128)S(1)} %get-tuple-element.24), channel_id=1, source_target_pairs={{1,0},{2,1},{3,2},{5,4},{6,5},{7,6},{9,8},{10,9},{11,10},{13,12},{... | collective-permute-start | bytes 92168 | tf_op jit(solution)/shard_map/ppermute | solution.py:22
  105.0 5.2 %collective-permute-start.7 = (f32[3,10,1,256]{3,2,1,0:T(1,128)S(1)}, f32[3,10,1,256]{3,2,1,0:T(1,128)S(1)}, u32[]{:S(2)}, u32[]{:S(2)}) collective-permute-start(f32[3,10,1,256]{3,2,1,0:T(1,128)S(1)} %get-tuple-element.23), channel_id=1, source_target_pairs={{0,1},{1,2},{2,3},{4,5},{5,6},{6,7},{8,9},{9,10},{10,11},{12,13},{... | collective-permute-start | bytes 92168 | tf_op jit(solution)/shard_map/ppermute | solution.py:21
  110.8 0.9 copy-start.4
  110.8 24.9 %copy-start.9 = (s32[1,128]{1,0:T(1,128)S(1)}, s32[1,128]{1,0:T(1,128)}, u32[]{:S(2)}) copy-start(s32[1,128]{1,0:T(1,128)} %param.21) | copy-start | bytes 1540
  110.8 25.0 %copy-start.8 = (f32[1,128]{1,0:T(1,128)S(1)}, f32[1,128]{1,0:T(1,128)}, u32[]{:S(2)}) copy-start(f32[1,128]{1,0:T(1,128)} %param.20) | copy-start | bytes 1540
  111.7 24.6 %copy-start.2 = (f32[3,8,16,256]{3,2,1,0:T(8,128)}, f32[3,8,16,256]{3,2,1,0:T(8,128)S(1)}, u32[]{:S(2)}) copy-start(f32[3,8,16,256]{3,2,1,0:T(8,128)S(1)} %fusion.18) | copy-start | bytes 1179652
where the time goes:
time: 137 us; the launch traced here: 136 us
  blocking collectives  59.4 us (43%)
  other arithmetic  35.8 us (26%)
  starting transfers between devices  25.2 us (18%)
  local copies, waits for them, and re-layouts  7.59 us (6%)
  waiting for transfers between devices  6.56 us (5%)
  between operations  1.76 us (1%)
    all_gather x1, blocking collectives, per_device(): lax.all_gather(own_wake, 'blk', axis=1, tiled=True)  30.7 us
    scatter-add x1, other arithmetic, per_device(): face = jnp.zeros((3, depth_y, depth_z), jnp.float32).at[:, jnp.clip(local...  25.4 us
    unnamed x1, blocking collectives  22.8 us
    ppermute x4, starting transfers between devices, with_halo(): before = lax.ppermute(last, axis, up)  13.3 us
    ppermute x4, starting transfers between devices, with_halo(): after = lax.ppermute(leading, axis, down)  6.43 us
    psum x1, blocking collectives, per_device(): velocity = lax.psum(partial_value, 'blade')  5.88 us
    all_to_all x1, starting transfers between devices, per_device(): lax.all_to_all(outgoing, 'blk', split_axis=1, concat_axis=1, tiled=True)  5.46 us
    ppermute x4, waiting for transfers between devices, with_halo(): before = lax.ppermute(last, axis, up)  5.2 us
  transfers between devices with their start and end apart: 9, of which 5 were waited for; matrix products, arithmetic and copies ran while one was open for 21% of the time, Pallas kernels for 0%

commit v1 on v0

--- a/solution.py
+++ b/solution.py
@@ -9,6 +9,22 @@
 FOUR_PI = 4.0 * math.pi
 OMEGA = 0.8
 RELAX = 0.5
+
+
+def collect(x, axis, dim):
+    ways, here, step = (lax.axis_size(axis), lax.axis_index(axis), x.shape[dim])
+    shape = [n * ways if d == dim else n for d, n in enumerate(x.shape)]
+    full = lax.dynamic_update_slice_in_dim(jnp.zeros(shape, x.dtype), x, here * step, axis=dim)
+    going_up = going_down = x
+    for far in range(1, ways // 2 + 1):
+        going_up = lax.ppermute(going_up, axis, [(d, (d + 1) % ways) for d in range(ways)])
+        full = lax.dynamic_update_slice_in_dim(full, going_up, (here - far) % ways * step, axis=dim)
+        if 2 * far < ways:
+            going_down = lax.ppermute(going_down, axis, [(d, (d - 1) % ways) for d in range(ways)])
+            full = lax.dynamic_update_slice_in_dim(
+                full, going_down, (here + far) % ways * step, axis=dim
+            )
+    return full
 
 
 def with_halo(array, sides, width):
@@ -90,7 +106,7 @@
     depth_y = flow.shape[2]
     depth_z = flow.shape[3]
     own_wake = jnp.concatenate([seg_start[:, 0], seg_step[:, 0], seg_gamma], 0)
-    partial_value = spanned(bnd_pos, lax.all_gather(own_wake, "blk", axis=1, tiled=True), 2048)
+    partial_value = spanned(bnd_pos, collect(own_wake, "blk", 1), 2048)
     velocity = lax.psum(partial_value, "blade")
     owner = bnd_owner[:, 0]
     onehot = (owner[:, None] == jnp.arange(n_blk, dtype=jnp.int32)[None, :]).astype(jnp.int32)

time: 137 us -> 128 us (0.934)
  blocking collectives: 59.4 us -> 25 us
  waiting for transfers between devices: 6.56 us -> 20.5 us
  starting transfers between devices: 25.2 us -> 36.2 us
    all_gather x1 -> x0, blocking collectives: 30.7 us -> none  [per_device(): lax.all_gather(own_wake, 'blk', axis=1, tiled=True)]
    ppermute x0 -> x7, starting transfers between devices: none -> 14.5 us  [the longest x3 10.2 us: collect(): lax.ppermute(going_down, axis, [(d, (d - 1) % ways) for d in range(ways)])]
    ppermute x0 -> x7, waiting for transfers between devices: none -> 9.56 us  [the longest x4 9.29 us: collect(): lax.ppermute(going_up, axis, [(d, (d + 1) % ways) for d in range(ways)])]
    all_to_all x1, waiting for transfers between devices: 1.23 us -> 6.42 us  [per_device(): lax.all_to_all(outgoing, 'blk', split_axis=1, concat_axis=1, tiled=True)]
    unnamed x1, blocking collectives: 22.8 us -> 19.1 us
    ppermute x4, starting transfers between devices: 13.3 us -> 9.67 us  [with_halo(): before = lax.ppermute(last, axis, up)]
    ppermute x4, starting transfers between devices: 6.43 us -> 8.74 us  [with_halo(): after = lax.ppermute(leading, axis, down)]
    ppermute x4, waiting for transfers between devices: 5.2 us -> 2.92 us  [with_halo(): before = lax.ppermute(last, axis, up)]
  transfers between devices with their start and end apart: 9 -> 16, of which waited for: 5 -> 9; matrix products, arithmetic and copies ran while one was open for 21% -> 29% of each run, Pallas kernels for 0% -> 0%
where the time goes in v1:
time: 128 us; the launch traced here: 127 us
  starting transfers between devices  36.2 us (28%)
  other arithmetic  34.9 us (27%)
  blocking collectives  25 us (20%)
  waiting for transfers between devices  20.5 us (16%)
  local copies, waits for them, and re-layouts  8.38 us (7%)
  between operations  1.96 us (2%)
    scatter-add x1, other arithmetic, per_device(): face = jnp.zeros((3, depth_y, depth_z), jnp.float32).at[:, jnp.clip(local...  25.4 us
    unnamed x1, blocking collectives  19.1 us
    ppermute x3, starting transfers between devices, collect(): lax.ppermute(going_down, axis, [(d, (d - 1) % ways) for d in range(ways)])  10.2 us
    ppermute x4, starting transfers between devices, with_halo(): before = lax.ppermute(last, axis, up)  9.67 us
    ppermute x4, waiting for transfers between devices, collect(): lax.ppermute(going_up, axis, [(d, (d + 1) % ways) for d in range(ways)])  9.29 us
    ppermute x4, starting transfers between devices, with_halo(): after = lax.ppermute(leading, axis, down)  8.74 us
    all_to_all x1, waiting for transfers between devices, per_device(): lax.all_to_all(outgoing, 'blk', split_axis=1, concat_axis=1, tiled=True)  6.42 us
    psum x1, blocking collectives, per_device(): velocity = lax.psum(partial_value, 'blade')  5.88 us
  transfers between devices with their start and end apart: 16, of which 9 were waited for; matrix products, arithmetic and copies ran while one was open for 29% of the time, Pallas kernels for 0%

profile of v1, /device:TPU:4, one launch (start us, length us, event | category | flops | bytes accessed | tf_op | source)
XLA Modules:
  0.0 127.1 jit_solution(14525974584584453167)
XLA Ops:
  2.0 1.5 %collective-permute-start = (f32[7,128]{1,0:T(8,128)S(1)}, f32[7,128]{1,0:T(8,128)S(1)}, u32[]{:S(2)}, u32[]{:S(2)}) collective-permute-start(f32[7,128]{1,0:T(8,128)S(1)} %get-tuple-element.24), channel_id=1, source_target_pairs={{0,4},{4,8},{8,12},{12,16},{16,20},{20,24},{24,28},{28,0},{1,5},{5... | collective-permute-start | bytes 10760 | tf_op jit(solution)/shard_map/ppermute | solution.py:20
  3.5 3.2 %collective-permute-start.1 = (f32[7,128]{1,0:T(8,128)S(1)}, f32[7,128]{1,0:T(8,128)S(1)}, u32[]{:S(2)}, u32[]{:S(2)}) collective-permute-start(f32[7,128]{1,0:T(8,128)S(1)} %get-tuple-element.24), channel_id=1, source_target_pairs={{0,28},{4,0},{8,4},{12,8},{16,12},{20,16},{24,20},{28,24},{1,29},{... | collective-permute-start | bytes 10760 | tf_op jit(solution)/shard_map/ppermute | solution.py:23
  8.9 1.3 %collective-permute-start.7 = (f32[3,1,16,256]{3,2,1,0:T(8,128)S(1)}, f32[3,1,16,256]{3,2,1,0:T(8,128)S(1)}, u32[]{:S(2)}, u32[]{:S(2)}) collective-permute-start(f32[3,1,16,256]{3,2,1,0:T(8,128)S(1)} %get-tuple-element.31), channel_id=1, source_target_pairs={{4,0},{8,4},{12,8},{16,12},{20,16},{24,20},{28,24},{5,1},{9,5},{13... | collective-permute-start | bytes 147464 | tf_op jit(solution)/shard_map/ppermute | solution.py:38
  11.4 2.7 %collective-permute-start.2 = (f32[7,128]{1,0:T(8,128)S(1)}, f32[7,128]{1,0:T(8,128)S(1)}, u32[]{:S(2)}, u32[]{:S(2)}) collective-permute-start(f32[7,128]{1,0:T(8,128)S(1)} %collective-permute-done), channel_id=1, source_target_pairs={{0,4},{4,8},{8,12},{12,16},{16,20},{20,24},{24,28},{28,0},{1,5},{5... | collective-permute-start | bytes 10760 | tf_op jit(solution)/shard_map/ppermute | solution.py:20
  14.1 2.5 %collective-permute-start.3 = (f32[7,128]{1,0:T(8,128)S(1)}, f32[7,128]{1,0:T(8,128)S(1)}, u32[]{:S(2)}, u32[]{:S(2)}) collective-permute-start(f32[7,128]{1,0:T(8,128)S(1)} %collective-permute-done.1), channel_id=1, source_target_pairs={{0,28},{4,0},{8,4},{12,8},{16,12},{20,16},{24,20},{28,24},{1,29},{... | collective-permute-start | bytes 10760 | tf_op jit(solution)/shard_map/ppermute | solution.py:23
  16.6 1.5 %collective-permute-done.2 = f32[7,128]{1,0:T(8,128)S(1)} collective-permute-done((f32[7,128]{1,0:T(8,128)S(1)}, f32[7,128]{1,0:T(8,128)S(1)}, u32[]{:S(2)}, u32[]{:S(2)}) %collective-permute-start.2) | collective-permute-done | bytes 3616 | tf_op jit(solution)/shard_map/ppermute | solution.py:20
  18.4 4.5 %collective-permute-start.5 = (f32[7,128]{1,0:T(8,128)S(1)}, f32[7,128]{1,0:T(8,128)S(1)}, u32[]{:S(2)}, u32[]{:S(2)}) collective-permute-start(f32[7,128]{1,0:T(8,128)S(1)} %collective-permute-done.3), channel_id=1, source_target_pairs={{0,28},{4,0},{8,4},{12,8},{16,12},{20,16},{24,20},{28,24},{1,29},{... | collective-permute-start | bytes 10760 | tf_op jit(solution)/shard_map/ppermute | solution.py:23
  22.9 1.5 %collective-permute-done.4 = f32[7,128]{1,0:T(8,128)S(1)} collective-permute-done((f32[7,128]{1,0:T(8,128)S(1)}, f32[7,128]{1,0:T(8,128)S(1)}, u32[]{:S(2)}, u32[]{:S(2)}) %collective-permute-start.4) | collective-permute-done | bytes 3616 | tf_op jit(solution)/shard_map/ppermute | solution.py:20
  24.4 6.3 %collective-permute-done.6 = f32[7,128]{1,0:T(8,128)S(1)} collective-permute-done((f32[7,128]{1,0:T(8,128)S(1)}, f32[7,128]{1,0:T(8,128)S(1)}, u32[]{:S(2)}, u32[]{:S(2)}) %collective-permute-start.6) | collective-permute-done | bytes 3616 | tf_op jit(solution)/shard_map/ppermute | solution.py:20
  33.0 1.4 %fusion.9 = (f32[256,1024]{1,0:T(8,128)S(1)}, f32[1,256,1024]{2,1,0:T(8,128)S(1)}, f32[1,256,1024]{2,1,0:T(8,128)S(1)}, f32[1,256,1024]{2,1,0:T(8,128)S(1)}) fusion(f32[256,1024]{1,0:T(8,128)S(1)} %get-tuple-element.34, f32[1024]{0:T(1024)S(1)} %broadcast_multiply_fusion, f32[1024]{0:T(1024)S(1)} %bitcast.96, f32[3,256,1024]{2,1,0:T(8,128)S(1)} %get-tuple-element.33, ...), kind=kLoop, calls=%fused_computation.27 | loop fusion | flops 4980736 | bytes 11542528 | tf_op jit(solution)/shard_map/div | solution.py:58
  34.7 5.9 %psum.7 = f32[3,256]{1,0:T(4,128)S(1)} all-reduce(f32[3,256]{1,0:T(4,128)S(1)} %pad_maximum_fusion.16), channel_id=1, replica_groups=mesh['blk'=8,'blade'=4] {'blade'}, use_global_device_ids=true, to_apply=%region_10.11 | all-reduce | flops 768 | bytes 6144 | tf_op jit(solution)/shard_map/psum | solution.py:110
  42.8 3.3 %all-to-all-start = ((f32[8,1,256]{2,1,0:T(1,128)}), f32[8,1,256]{2,1,0:T(1,128)S(1)}, u32[]{:S(2)}, u32[]{:S(2)}) async-start(f32[8,1,256]{2,1,0:T(1,128)} %reshape.330), calls=%async_computation | async-start | bytes 16384 | tf_op jit(solution)/shard_map/all_to_all | solution.py:119
  46.2 6.4 %all-to-all-done = f32[8,1,256]{2,1,0:T(1,128)S(1)} async-done(((f32[8,1,256]{2,1,0:T(1,128)}), f32[8,1,256]{2,1,0:T(1,128)S(1)}, u32[]{:S(2)}, u32[]{:S(2)}) %all-to-all-start) | async-done | bytes 8224 | tf_op jit(solution)/shard_map/all_to_all | solution.py:119
  54.6 25.4 %scatter_fusion = f32[3,16,256]{0,2,1:T(8,128)S(1)} fusion(f32[3,16,256]{0,2,1:T(8,128)S(1)} %broadcast_in_dim.30, s32[512]{0:T(512)S(1)} %bitcast.90, f32[512,3]{1,0:T(8,128)S(1)} %copy.41), kind=kCustom, calls=%fused_computation.2 | custom fusion | flops 1536 | bytes 22528 | tf_op jit(solution)/shard_map/scatter-add | solution.py:131
  81.1 1.9 %collective-permute-start.10 = (f32[3,10,1,256]{3,2,1,0:T(1,128)S(1)}, f32[3,10,1,256]{3,2,1,0:T(1,128)S(1)}, u32[]{:S(2)}, u32[]{:S(2)}) collective-permute-start(f32[3,10,1,256]{3,2,1,0:T(1,128)S(1)} %get-tuple-element.27), channel_id=1, source_target_pairs={{0,1},{1,2},{2,3},{4,5},{5,6},{6,7},{8,9},{9,10},{10,11},{12,13},{... | collective-permute-start | bytes 92168 | tf_op jit(solution)/shard_map/ppermute | solution.py:37
  83.0 3.6 %collective-permute-start.9 = (f32[3,10,1,256]{3,2,1,0:T(1,128)S(1)}, f32[3,10,1,256]{3,2,1,0:T(1,128)S(1)}, u32[]{:S(2)}, u32[]{:S(2)}) collective-permute-start(f32[3,10,1,256]{3,2,1,0:T(1,128)S(1)} %get-tuple-element.28), channel_id=1, source_target_pairs={{1,0},{2,1},{3,2},{5,4},{6,5},{7,6},{9,8},{10,9},{11,10},{13,12},{... | collective-permute-start | bytes 92168 | tf_op jit(solution)/shard_map/ppermute | solution.py:38
  86.7 1.5 %collective-permute-done.9 = f32[3,10,1,256]{3,2,1,0:T(1,128)S(1)} collective-permute-done((f32[3,10,1,256]{3,2,1,0:T(1,128)S(1)}, f32[3,10,1,256]{3,2,1,0:T(1,128)S(1)}, u32[]{:S(2)}, u32[]{:S(2)}) %collective-permute-start.9) | collective-permute-done | bytes 30752 | tf_op jit(solution)/shard_map/ppermute | solution.py:38
  89.2 1.3 %collective-permute-start.11 = (f32[3,1,16,256]{3,2,1,0:T(8,128)S(1)}, f32[3,1,16,256]{3,2,1,0:T(8,128)S(1)}, u32[]{:S(2)}, u32[]{:S(2)}) collective-permute-start(f32[3,1,16,256]{3,2,1,0:T(8,128)S(1)} %get-tuple-element.30), channel_id=1, source_target_pairs={{4,0},{8,4},{12,8},{16,12},{20,16},{24,20},{28,24},{5,1},{9,5},{13... | collective-permute-start | bytes 147464 | tf_op jit(solution)/shard_map/ppermute | solution.py:38
  90.5 4.5 %collective-permute-start.12 = (f32[3,1,16,256]{3,2,1,0:T(8,128)S(1)}, f32[3,1,16,256]{3,2,1,0:T(8,128)S(1)}, u32[]{:S(2)}, u32[]{:S(2)}) collective-permute-start(f32[3,1,16,256]{3,2,1,0:T(8,128)S(1)} %get-tuple-element.29), channel_id=1, source_target_pairs={{0,4},{4,8},{8,12},{12,16},{16,20},{20,24},{24,28},{1,5},{5,9},{9,... | collective-permute-start | bytes 147464 | tf_op jit(solution)/shard_map/ppermute | solution.py:37
  95.2 1.6 %collective-permute-done.12 = f32[3,1,16,256]{3,2,1,0:T(8,128)S(1)} collective-permute-done((f32[3,1,16,256]{3,2,1,0:T(8,128)S(1)}, f32[3,1,16,256]{3,2,1,0:T(8,128)S(1)}, u32[]{:S(2)}, u32[]{:S(2)}) %collective-permute-start.12) | collective-permute-done | bytes 49184 | tf_op jit(solution)/shard_map/ppermute | solution.py:37
  96.9 2.5 %collective-permute-start.13 = (f32[3,10,1,256]{3,2,1,0:T(1,128)S(1)}, f32[3,10,1,256]{3,2,1,0:T(1,128)S(1)}, u32[]{:S(2)}, u32[]{:S(2)}) collective-permute-start(f32[3,10,1,256]{3,2,1,0:T(1,128)S(1)} %get-tuple-element.26), channel_id=1, source_target_pairs={{1,0},{2,1},{3,2},{5,4},{6,5},{7,6},{9,8},{10,9},{11,10},{13,12},{... | collective-permute-start | bytes 92168 | tf_op jit(solution)/shard_map/ppermute | solution.py:38
  99.4 1.9 %collective-permute-start.14 = (f32[3,10,1,256]{3,2,1,0:T(1,128)S(1)}, f32[3,10,1,256]{3,2,1,0:T(1,128)S(1)}, u32[]{:S(2)}, u32[]{:S(2)}) collective-permute-start(f32[3,10,1,256]{3,2,1,0:T(1,128)S(1)} %get-tuple-element.25), channel_id=1, source_target_pairs={{0,1},{1,2},{2,3},{4,5},{5,6},{6,7},{8,9},{9,10},{10,11},{12,13},{... | collective-permute-start | bytes 92168 | tf_op jit(solution)/shard_map/ppermute | solution.py:37
  103.3 1.3 %collective-permute-done.14 = f32[3,10,1,256]{3,2,1,0:T(1,128)S(1)} collective-permute-done((f32[3,10,1,256]{3,2,1,0:T(1,128)S(1)}, f32[3,10,1,256]{3,2,1,0:T(1,128)S(1)}, u32[]{:S(2)}, u32[]{:S(2)}) %collective-permute-start.14) | collective-permute-done | bytes 30752 | tf_op jit(solution)/shard_map/ppermute | solution.py:37
  106.5 19.1 %all-reduce.2 = f32[128]{0:T(128)S(1)} all-reduce(f32[128]{0:T(128)S(1)} %dynamic-update-slice.3), channel_id=2, replica_groups=mesh['blk'=8,'blade'=4] {'blk'}, use_global_device_ids=true, to_apply=%add.2 | all-reduce | flops 128 | bytes 1024
  (104 shorter events, 18.3 us)
Async XLA Ops:
  0.6 30.1 %copy-start.5 = (f32[3,256]{1,0:T(4,128)S(1)}, f32[3,256]{1,0:T(4,128)}, u32[]{:S(2)}) copy-start(f32[3,256]{1,0:T(4,128)} %param.15) | copy-start | bytes 9220
  0.6 9.6 %copy-start.6 = (s32[256,1]{0,1:T(1,128)S(1)}, s32[256,1]{0,1:T(1,128)}, u32[]{:S(2)}) copy-start(s32[256,1]{0,1:T(1,128)} %param.16) | copy-start | bytes 3076
  0.7 10.6 %copy-start.7 = (s32[256]{0:T(256)S(1)}, s32[256]{0:T(256)}, u32[]{:S(2)}) copy-start(s32[256]{0:T(256)} %param.17) | copy-start | bytes 3076
  2.0 9.3 %collective-permute-start = (f32[7,128]{1,0:T(8,128)S(1)}, f32[7,128]{1,0:T(8,128)S(1)}, u32[]{:S(2)}, u32[]{:S(2)}) collective-permute-start(f32[7,128]{1,0:T(8,128)S(1)} %get-tuple-element.24), channel_id=1, source_target_pairs={{0,4},{4,8},{8,12},{12,16},{16,20},{20,24},{24,28},{28,0},{1,5},{5... | collective-permute-start | bytes 10760 | tf_op jit(solution)/shard_map/ppermute | solution.py:20
  3.5 10.5 %collective-permute-start.1 = (f32[7,128]{1,0:T(8,128)S(1)}, f32[7,128]{1,0:T(8,128)S(1)}, u32[]{:S(2)}, u32[]{:S(2)}) collective-permute-start(f32[7,128]{1,0:T(8,128)S(1)} %get-tuple-element.24), channel_id=1, source_target_pairs={{0,28},{4,0},{8,4},{12,8},{16,12},{20,16},{24,20},{28,24},{1,29},{... | collective-permute-start | bytes 10760 | tf_op jit(solution)/shard_map/ppermute | solution.py:23
  7.6 73.0 %collective-permute-start.8 = (f32[3,1,16,256]{3,2,1,0:T(8,128)S(1)}, f32[3,1,16,256]{3,2,1,0:T(8,128)S(1)}, u32[]{:S(2)}, u32[]{:S(2)}) collective-permute-start(f32[3,1,16,256]{3,2,1,0:T(8,128)S(1)} %get-tuple-element.32), channel_id=1, source_target_pairs={{0,4},{4,8},{8,12},{12,16},{16,20},{20,24},{24,28},{1,5},{5,9},{9,... | collective-permute-start | bytes 147464 | tf_op jit(solution)/shard_map/ppermute | solution.py:37
  8.9 72.1 %collective-permute-start.7 = (f32[3,1,16,256]{3,2,1,0:T(8,128)S(1)}, f32[3,1,16,256]{3,2,1,0:T(8,128)S(1)}, u32[]{:S(2)}, u32[]{:S(2)}) collective-permute-start(f32[3,1,16,256]{3,2,1,0:T(8,128)S(1)} %get-tuple-element.31), channel_id=1, source_target_pairs={{4,0},{8,4},{12,8},{16,12},{20,16},{24,20},{28,24},{5,1},{9,5},{13... | collective-permute-start | bytes 147464 | tf_op jit(solution)/shard_map/ppermute | solution.py:38
  11.4 6.7 %collective-permute-start.2 = (f32[7,128]{1,0:T(8,128)S(1)}, f32[7,128]{1,0:T(8,128)S(1)}, u32[]{:S(2)}, u32[]{:S(2)}) collective-permute-start(f32[7,128]{1,0:T(8,128)S(1)} %collective-permute-done), channel_id=1, source_target_pairs={{0,4},{4,8},{8,12},{12,16},{16,20},{20,24},{24,28},{28,0},{1,5},{5... | collective-permute-start | bytes 10760 | tf_op jit(solution)/shard_map/ppermute | solution.py:20
  14.1 4.3 %collective-permute-start.3 = (f32[7,128]{1,0:T(8,128)S(1)}, f32[7,128]{1,0:T(8,128)S(1)}, u32[]{:S(2)}, u32[]{:S(2)}) collective-permute-start(f32[7,128]{1,0:T(8,128)S(1)} %collective-permute-done.1), channel_id=1, source_target_pairs={{0,28},{4,0},{8,4},{12,8},{16,12},{20,16},{24,20},{28,24},{1,29},{... | collective-permute-start | bytes 10760 | tf_op jit(solution)/shard_map/ppermute | solution.py:23
  18.1 6.3 %collective-permute-start.4 = (f32[7,128]{1,0:T(8,128)S(1)}, f32[7,128]{1,0:T(8,128)S(1)}, u32[]{:S(2)}, u32[]{:S(2)}) collective-permute-start(f32[7,128]{1,0:T(8,128)S(1)} %collective-permute-done.2), channel_id=1, source_target_pairs={{0,4},{4,8},{8,12},{12,16},{16,20},{20,24},{24,28},{28,0},{1,5},{5... | collective-permute-start | bytes 10760 | tf_op jit(solution)/shard_map/ppermute | solution.py:20
  18.4 6.0 %collective-permute-start.5 = (f32[7,128]{1,0:T(8,128)S(1)}, f32[7,128]{1,0:T(8,128)S(1)}, u32[]{:S(2)}, u32[]{:S(2)}) collective-permute-start(f32[7,128]{1,0:T(8,128)S(1)} %collective-permute-done.3), channel_id=1, source_target_pairs={{0,28},{4,0},{8,4},{12,8},{16,12},{20,16},{24,20},{28,24},{1,29},{... | collective-permute-start | bytes 10760 | tf_op jit(solution)/shard_map/ppermute | solution.py:23
  24.4 6.3 %collective-permute-start.6 = (f32[7,128]{1,0:T(8,128)S(1)}, f32[7,128]{1,0:T(8,128)S(1)}, u32[]{:S(2)}, u32[]{:S(2)}) collective-permute-start(f32[7,128]{1,0:T(8,128)S(1)} %collective-permute-done.4), channel_id=1, source_target_pairs={{0,4},{4,8},{8,12},{12,16},{16,20},{20,24},{24,28},{28,0},{1,5},{5... | collective-permute-start | bytes 10760 | tf_op jit(solution)/shard_map/ppermute | solution.py:20
  34.3 11.8 %copy-start.3 = (f32[8,16,256]{2,1,0:T(8,128)S(1)}, f32[8,16,256]{2,1,0:T(8,128)}, u32[]{:S(2)}) copy-start(f32[8,16,256]{2,1,0:T(8,128)} %param.24) | copy-start | bytes 393220
  42.8 9.8 %all-to-all-start = ((f32[8,1,256]{2,1,0:T(1,128)}), f32[8,1,256]{2,1,0:T(1,128)S(1)}, u32[]{:S(2)}, u32[]{:S(2)}) async-start(f32[8,1,256]{2,1,0:T(1,128)} %reshape.330), calls=%async_computation | async-start | bytes 16384 | tf_op jit(solution)/shard_map/all_to_all | solution.py:119
  81.1 5.6 %collective-permute-start.10 = (f32[3,10,1,256]{3,2,1,0:T(1,128)S(1)}, f32[3,10,1,256]{3,2,1,0:T(1,128)S(1)}, u32[]{:S(2)}, u32[]{:S(2)}) collective-permute-start(f32[3,10,1,256]{3,2,1,0:T(1,128)S(1)} %get-tuple-element.27), channel_id=1, source_target_pairs={{0,1},{1,2},{2,3},{4,5},{5,6},{6,7},{8,9},{9,10},{10,11},{12,13},{... | collective-permute-start | bytes 92168 | tf_op jit(solution)/shard_map/ppermute | solution.py:37
  83.0 5.2 %collective-permute-start.9 = (f32[3,10,1,256]{3,2,1,0:T(1,128)S(1)}, f32[3,10,1,256]{3,2,1,0:T(1,128)S(1)}, u32[]{:S(2)}, u32[]{:S(2)}) collective-permute-start(f32[3,10,1,256]{3,2,1,0:T(1,128)S(1)} %get-tuple-element.28), channel_id=1, source_target_pairs={{1,0},{2,1},{3,2},{5,4},{6,5},{7,6},{9,8},{10,9},{11,10},{13,12},{... | collective-permute-start | bytes 92168 | tf_op jit(solution)/shard_map/ppermute | solution.py:38
  88.8 13.2 %copy-start.10 = (u32[32]{0:T(128)S(1)}, u32[32]{0:T(128)}, u32[]{:S(2)}) copy-start(u32[32]{0:T(128)} %constant.202) | copy-start | bytes 388
  89.2 6.0 %collective-permute-start.11 = (f32[3,1,16,256]{3,2,1,0:T(8,128)S(1)}, f32[3,1,16,256]{3,2,1,0:T(8,128)S(1)}, u32[]{:S(2)}, u32[]{:S(2)}) collective-permute-start(f32[3,1,16,256]{3,2,1,0:T(8,128)S(1)} %get-tuple-element.30), channel_id=1, source_target_pairs={{4,0},{8,4},{12,8},{16,12},{20,16},{24,20},{28,24},{5,1},{9,5},{13... | collective-permute-start | bytes 147464 | tf_op jit(solution)/shard_map/ppermute | solution.py:38
  90.5 6.3 %collective-permute-start.12 = (f32[3,1,16,256]{3,2,1,0:T(8,128)S(1)}, f32[3,1,16,256]{3,2,1,0:T(8,128)S(1)}, u32[]{:S(2)}, u32[]{:S(2)}) collective-permute-start(f32[3,1,16,256]{3,2,1,0:T(8,128)S(1)} %get-tuple-element.29), channel_id=1, source_target_pairs={{0,4},{4,8},{8,12},{12,16},{16,20},{20,24},{24,28},{1,5},{5,9},{9,... | collective-permute-start | bytes 147464 | tf_op jit(solution)/shard_map/ppermute | solution.py:37
  96.9 6.4 %collective-permute-start.13 = (f32[3,10,1,256]{3,2,1,0:T(1,128)S(1)}, f32[3,10,1,256]{3,2,1,0:T(1,128)S(1)}, u32[]{:S(2)}, u32[]{:S(2)}) collective-permute-start(f32[3,10,1,256]{3,2,1,0:T(1,128)S(1)} %get-tuple-element.26), channel_id=1, source_target_pairs={{1,0},{2,1},{3,2},{5,4},{6,5},{7,6},{9,8},{10,9},{11,10},{13,12},{... | collective-permute-start | bytes 92168 | tf_op jit(solution)/shard_map/ppermute | solution.py:38
  99.4 5.2 %collective-permute-start.14 = (f32[3,10,1,256]{3,2,1,0:T(1,128)S(1)}, f32[3,10,1,256]{3,2,1,0:T(1,128)S(1)}, u32[]{:S(2)}, u32[]{:S(2)}) collective-permute-start(f32[3,10,1,256]{3,2,1,0:T(1,128)S(1)} %get-tuple-element.25), channel_id=1, source_target_pairs={{0,1},{1,2},{2,3},{4,5},{5,6},{6,7},{8,9},{9,10},{10,11},{12,13},{... | collective-permute-start | bytes 92168 | tf_op jit(solution)/shard_map/ppermute | solution.py:37
  105.2 21.2 %copy-start.9 = (s32[1,128]{1,0:T(1,128)S(1)}, s32[1,128]{1,0:T(1,128)}, u32[]{:S(2)}) copy-start(s32[1,128]{1,0:T(1,128)} %param.21) | copy-start | bytes 1540
  105.2 21.3 %copy-start.8 = (f32[1,128]{1,0:T(1,128)S(1)}, f32[1,128]{1,0:T(1,128)}, u32[]{:S(2)}) copy-start(f32[1,128]{1,0:T(1,128)} %param.20) | copy-start | bytes 1540
  106.1 21.0 %copy-start.2 = (f32[3,8,16,256]{3,2,1,0:T(8,128)}, f32[3,8,16,256]{3,2,1,0:T(8,128)S(1)}, u32[]{:S(2)}) copy-start(f32[3,8,16,256]{3,2,1,0:T(8,128)S(1)} %fusion.18) | copy-start | bytes 1179652
  (3 other events, 8.6 us)
